TPU v7x, 128 devices: a whole 4x4x4 slice. The times are simulated.
128 devices in a mesh: row: 16 (over x, y), col: 8 (over z, core).
Axes of the slice: x: 4, y: 4, z: 4, core: 2. Of those that a mesh axis runs over, the one named last changes fastest.
Arguments:
- object_slab: float32 [4, 4096, 4096], P(None, 'row', 'col'), may hold values from -6 to 6
- probe_wave: float32 [2, 256, 256], replicated, may hold values from -6 to 6
- scan_offsets: int32 [1024, 2], P(('row', 'col')), may hold values from 0 to 3840, as said below
- live_counts: int32 [128], P(('row', 'col')), may hold values from 1 to 8, as said below
- amplitudes: float32 [1024, 256, 256], P(('row', 'col')), may hold values from 0 to 3
Outputs:
- object_grad: float32 [4, 4096, 4096], P(None, 'row', 'col')
- probe_grad: float32 [2, 256, 256], replicated
Inputs may be any that keep to these rules, and one draw needn't show every extreme that they name: `scan_offsets`: each slot's window lies inside the object, and its corner lies in the object tile of the device that holds the slot. Slot 0 of the first device has corner (0, 0), slot 0 of the last device has corner (3840, 3840). `live_counts`: every device has at least one live slot and some device has all 8 slots live.
All inputs are finite; a program needn't handle non-finite values.
Results may differ from a plain program's by a relative error of at most 0.0003.
Values sent between devices are 32-bit elements; how exact they have to be, the bound alone decides.
No kernel may reach another device: no remote copies, remote signals or barrier semaphores. Data moves between devices by JAX's collectives and lax.ppermute only.
A program may use at most 128 MiB of HBM per device.

v0:
```python
import math

import jax
import jax.numpy as jnp
from jax import lax
from jax.sharding import PartitionSpec as P


def from_behind(value, axis, steps):
    count = lax.axis_size(axis)
    first, last = (max(0, -steps), min(count, count - steps))
    return lax.ppermute(value, axis, [(source, source + steps) for source in range(first, last)])


def fresnel_phase(width):
    index_range = jnp.arange(width)
    freqs = (
        jnp.where(index_range < width // 2, index_range, index_range - width).astype(jnp.float32)
        / width
    )
    square_sum = freqs[:, None] ** 2 + freqs[None, :] ** 2
    return -math.pi * (width / 4.0) * square_sum


def dft_tables(width):
    index_range = jnp.arange(width)
    products = index_range[:, None] * index_range[None, :] % width
    angles = 2.0 * math.pi / width * products.astype(jnp.float32)
    norm_scale = 1.0 / math.sqrt(width)
    return (jnp.cos(angles) * norm_scale, -jnp.sin(angles) * norm_scale)


def real_dot(left, right):
    return jnp.dot(left, right, precision=lax.Precision.HIGHEST, preferred_element_type=jnp.float32)


def complex_dot(left, right):
    return (
        real_dot(left[0], right[0]) - real_dot(left[1], right[1]),
        real_dot(left[0], right[1]) + real_dot(left[1], right[0]),
    )


def complex_mul(left, right):
    return (left[0] * right[0] - left[1] * right[1], left[0] * right[1] + left[1] * right[0])


def conjugate(field):
    return (field[0], -field[1])


def transform(field, table):
    return complex_dot(complex_dot(table, field), table)


def position_grads(window, measured, probe_wave, forward, inverse, transfer):
    object_one = (window[0], window[1])
    object_two = (window[2], window[3])
    probe_field = (probe_wave[0], probe_wave[1])
    psi_one = complex_mul(probe_field, object_one)
    propagated = transform(complex_mul(transfer, transform(psi_one, forward)), inverse)
    psi_two = complex_mul(propagated, object_two)
    far_field = transform(psi_two, forward)
    intensity = far_field[0] * far_field[0] + far_field[1] * far_field[1]
    factor = 1.0 - measured / jnp.sqrt(intensity + 1.0)
    residue_wave = (factor * far_field[0], factor * far_field[1])
    back_far = transform(residue_wave, inverse)
    grad_two = complex_mul(conjugate(propagated), back_far)
    back_prop = complex_mul(conjugate(object_two), back_far)
    back_one = transform(complex_mul(conjugate(transfer), transform(back_prop, forward)), inverse)
    grad_one = complex_mul(conjugate(probe_field), back_one)
    grad_probe = complex_mul(conjugate(object_one), back_one)
    object_part = jnp.stack([grad_one[0], grad_one[1], grad_two[0], grad_two[1]])
    probe_part = jnp.stack([grad_probe[0], grad_probe[1]])
    return (object_part, probe_part)


def body(object_slab, probe_wave, scan_offsets, live_counts, amplitudes):
    width = probe_wave.shape[1]
    rows_tile = object_slab.shape[1]
    cols_tile = object_slab.shape[2]
    slots = scan_offsets.shape[0]
    right_strip = from_behind(object_slab[:, :, :width], "col", -1)
    widened = jnp.concatenate([object_slab, right_strip], axis=2)
    down_strip = from_behind(widened, "row", -1)
    extended = jnp.concatenate([widened, down_strip], axis=1)
    local_rows = scan_offsets[:, 0] - lax.axis_index("row") * rows_tile
    local_cols = scan_offsets[:, 1] - lax.axis_index("col") * cols_tile
    live_count = live_counts[0]
    zero_index = jnp.zeros((), jnp.int32)
    forward = dft_tables(width)
    inverse = (forward[0], -forward[1])
    phases = fresnel_phase(width)
    transfer = (jnp.cos(phases), jnp.sin(phases))

    def window_at(slot):
        return lax.dynamic_slice(
            extended, (zero_index, local_rows[slot], local_cols[slot]), (4, width, width)
        )

    def add_window(grad_ext, piece, slot):
        start = (zero_index, local_rows[slot], local_cols[slot])
        current = lax.dynamic_slice(grad_ext, start, (4, width, width))
        return lax.dynamic_update_slice(grad_ext, current + piece, start)

    def visit(slot, carry):

        def active(state):
            grad_ext, probe_acc = state
            object_part, probe_part = position_grads(
                window_at(slot), amplitudes[slot], probe_wave, forward, inverse, transfer
            )
            return (add_window(grad_ext, object_part, slot), probe_acc + probe_part)

        return lax.cond(slot < live_count, active, lambda state: state, carry)

    grad_init = jnp.zeros_like(extended)
    probe_init = jnp.zeros_like(probe_wave)
    grad_ext, probe_acc = lax.fori_loop(0, slots, visit, (grad_init, probe_init))
    right_back = from_behind(grad_ext[:, :, cols_tile:], "col", 1)
    grad_ext = grad_ext[:, :, :cols_tile].at[:, :, :width].add(right_back)
    down_back = from_behind(grad_ext[:, rows_tile:, :], "row", 1)
    object_grad = grad_ext[:, :rows_tile, :].at[:, :width, :].add(down_back)
    probe_grad = lax.psum(probe_acc, ("row", "col"))
    return (object_grad, probe_grad)


def solution(mesh):
    return jax.shard_map(
        body,
        mesh=mesh,
        in_specs=(
            P(None, "row", "col"),
            P(),
            P(("row", "col"), None),
            P(("row", "col")),
            P(("row", "col"), None, None),
        ),
        out_specs=(P(None, "row", "col"), P()),
        check_vma=False,
    )
```

profile of v0, /device:TPU:6, one launch (start us, length us, event | category | flops | bytes accessed | tf_op | source)
XLA Modules:
  0.0 766.4 jit_solution(15608679540647583829)
XLA Ops:
  7.2 1.4 slice.85
  8.7 1.3 collective-permute-start
  10.0 1.5 constant_dynamic-update-slice_fusion.1
  11.5 1.7 collective-permute-done
  13.2 1.1 constant_dynamic-update-slice_fusion
  14.3 5.2 collective-permute-start.1
  19.5 57.4 %collective-permute-done.1 = f32[4,256,768]{2,1,0:T(8,128)} collective-permute-done((f32[4,256,768]{2,1,0:T(8,128)}, f32[4,256,768]{2,1,0:T(8,128)}, u32[]{:S(2)}, u32[]{:S(2)}) %collective-permute-start.1) | collective-permute-done | bytes 3145760 | tf_op jit(solution)/shard_map/ppermute | solution.py:12
  76.9 6.1 pad_maximum_fusion
  83.0 3.1 broadcast_in_dim.4
  86.2 130.7 %while.21 = (s32[]{:T(128)}, f32[4,512,768]{2,1,0:T(8,128)}, f32[2,256,256]{2,1,0:T(8,128)S(1)}, s32[]{:T(128)}, s32[8]{0:T(128)S(1)}, /*index=5*/s32[8]{0:T(128...) while((s32[]{:T(128)}, f32[4,512,768]{2,1,0:T(8,128)}, ...), condition=%wide.region_3.4_spmd.clone.clone.clone, body=%wide.region_0.3_spmd.clone.clone.clone.sunk | while | flops 9673506816 | bytes 63702624 | solution.py:119
  86.4 1.0 negate_multiply_fusion.2
  88.1 56.6 %conditional.5 = ((f32[4,512,768]{2,1,0:T(8,128)}, f32[2,256,256]{2,1,0:T(8,128)S(1)})) conditional(s32[]{:T(128)} %convert_element_type.164, (f32[4,512,768]{2,1,0:T(8,128)}, f32[2,256,256]{2,1,0:T(8,128)S(1)}) %tuple.127, (s32[]{:T(128)}, s32[8]{0:T(128)S(1)}, s32[8]{0:T(128)S(1)}, f32[4,512,768]{2,1,0:T(8,128)}, ...), branch_computations={%region_1.1_spmd, %region_2.2_spmd.clone} | conditional | flops 9671409664 | bytes 62652672 | solution.py:115
  88.1 0.6 dynamic_slice.17
  90.5 0.6 dynamic_slice.18
  93.0 2.1 fusion.11
  99.3 0.8 cos.72
  100.2 0.8 sin.76
  101.0 0.6 multiply_add_fusion.3
  102.2 0.6 convolution_add_fusion.9
  105.3 0.6 fusion.29
  105.9 1.8 multiply_add_fusion.2
  111.9 1.6 fusion.17
  114.1 0.6 convolution_subtract_fusion.5
  117.8 1.9 multiply_add_fusion.1
  123.9 0.6 multiply_add_fusion
  127.5 0.6 fusion.19
  128.8 1.9 subtract_bitcast_fusion
  130.8 1.8 maximum_add_fusion
  132.6 12.0 %dynamic_update_slice.3 = f32[4,512,768]{2,1,0:T(8,128)} dynamic-update-slice(f32[4,512,768]{2,1,0:T(8,128)} %get-tuple-element.730, f32[4,256,256]{2,1,0:T(8,128)S(1)} %maximum_add_fusion, s32[]{:T(128)} %constant.104.clone.1, s32[]{:T(128)S(6)} %select_n.162, s32[]{:T(128)S(6)} %select_n.163) | dynamic-update-slice | bytes 2097156 | tf_op jit(solution)/shard_map/while/body/eval_jaxpr/cond/branch_1_fun/dynamic_update_slice | solution.py:104
  144.8 1.0 negate_multiply_fusion.2
  146.5 56.7 %conditional.5 = ((f32[4,512,768]{2,1,0:T(8,128)}, f32[2,256,256]{2,1,0:T(8,128)S(1)})) conditional(s32[]{:T(128)} %convert_element_type.164, (f32[4,512,768]{2,1,0:T(8,128)}, f32[2,256,256]{2,1,0:T(8,128)S(1)}) %tuple.127, (s32[]{:T(128)}, s32[8]{0:T(128)S(1)}, s32[8]{0:T(128)S(1)}, f32[4,512,768]{2,1,0:T(8,128)}, ...), branch_computations={%region_1.1_spmd, %region_2.2_spmd.clone} | conditional | flops 9671409664 | bytes 62652672 | solution.py:115
  146.5 0.6 dynamic_slice.17
  148.9 0.6 dynamic_slice.18
  151.4 2.1 fusion.11
  157.7 0.8 cos.72
  158.6 0.8 sin.76
  159.4 0.6 multiply_add_fusion.3
  160.6 0.6 convolution_add_fusion.9
  164.3 1.8 multiply_add_fusion.2
  170.3 1.6 fusion.17
  172.5 0.6 convolution_subtract_fusion.5
  176.2 1.9 multiply_add_fusion.1
  182.3 0.6 multiply_add_fusion
  187.2 1.9 subtract_bitcast_fusion
  189.2 1.8 maximum_add_fusion
  191.0 12.1 %dynamic_update_slice.3 = f32[4,512,768]{2,1,0:T(8,128)} dynamic-update-slice(f32[4,512,768]{2,1,0:T(8,128)} %get-tuple-element.730, f32[4,256,256]{2,1,0:T(8,128)S(1)} %maximum_add_fusion, s32[]{:T(128)} %constant.104.clone.1, s32[]{:T(128)S(6)} %select_n.162, s32[]{:T(128)S(6)} %select_n.163) | dynamic-update-slice | bytes 2097156 | tf_op jit(solution)/shard_map/while/body/eval_jaxpr/cond/branch_1_fun/dynamic_update_slice | solution.py:104
  203.3 1.0 negate_multiply_fusion.2
  205.2 1.0 negate_multiply_fusion.2
  207.0 1.0 negate_multiply_fusion.2
  208.9 1.0 negate_multiply_fusion.2
  210.8 1.0 negate_multiply_fusion.2
  212.6 1.0 negate_multiply_fusion.2
  216.9 1.9 slice.88
  218.8 351.2 %collective-permute-start.2 = (f32[4,512,256]{2,1,0:T(8,128)S(1)}, f32[4,512,256]{2,1,0:T(8,128)S(1)}, u32[]{:S(2)}, u32[]{:S(2)}) collective-permute-start(f32[4,512,256]{2,1,0:T(8,128)S(1)} %slice.88), channel_id=1, source_target_pairs={{0,1},{1,2},{2,3},{3,4},{4,5},{5,6},{6,7},{8,9},{9,10},{10,11},{11... | collective-permute-start | bytes 6291464 | tf_op jit(solution)/shard_map/ppermute | solution.py:12
  570.1 2.6 slice.86
  572.7 1.0 collective-permute-done.2
  573.7 1.9 add_dynamic-update-slice_fusion
  575.6 1.9 copy-done.2
  577.5 1.5 slice.98
  579.0 2.0 collective-permute-start.3
  581.1 29.9 %collective-permute-done.3 = f32[4,256,512]{2,1,0:T(8,128)S(1)} collective-permute-done((f32[4,256,512]{2,1,0:T(8,128)}, f32[4,256,512]{2,1,0:T(8,128)S(1)}, u32[]{:S(2)}, u32[]{:S(2)}) %collective-permute-start.3) | collective-permute-done | bytes 2097184 | tf_op jit(solution)/shard_map/ppermute | solution.py:12
  610.9 3.4 slice_add_fusion
  614.3 143.0 %all-reduce.2.cloned.1.call-done = f32[2,256,256]{2,1,0:T(8,128)} async-done(((f32[2,256,256]{2,1,0:T(8,128)}), f32[2,256,256]{2,1,0:T(8,128)}) %all-reduce.2.cloned.1.call-update) | async-done | bytes 524304 | tf_op jit(solution)/shard_map/psum | solution.py:124
  757.4 1.9 copy.26
  (116 shorter events, 48.6 us)
Async XLA Ops:
  7.2 2.8 copy-start.3
  7.2 750.2 %all-reduce.2.cloned.1.call-start = ((), (), s32[]{:S(2)}) async-start(), calls=%async_computation | async-start | bytes 1048576 | tf_op jit(solution)/shard_map/psum | solution.py:124
  8.7 10.9 %copy-start.4 = (s32[8,2]{0,1:T(2,128)S(1)}, s32[8,2]{0,1:T(2,128)}, u32[]{:S(2)}) copy-start(s32[8,2]{0,1:T(2,128)} %param.17) | copy-start | bytes 196
  8.7 4.6 collective-permute-start
  14.3 62.6 %collective-permute-start.1 = (f32[4,256,768]{2,1,0:T(8,128)}, f32[4,256,768]{2,1,0:T(8,128)}, u32[]{:S(2)}, u32[]{:S(2)}) collective-permute-start(f32[4,256,768]{2,1,0:T(8,128)} %constant_dynamic-update-slice_fusion), channel_id=1, source_target_pairs={{8,0},{16,8},{24,16},{32,24},{40,32},{48,40},{56,48},{64,56},{72,6... | collective-permute-start | bytes 9437192 | tf_op jit(solution)/shard_map/ppermute | solution.py:12
  83.0 3.2 copy-start
  216.9 355.8 %copy-start.1 = (f32[2,256,256]{2,1,0:T(8,128)}, f32[2,256,256]{2,1,0:T(8,128)S(1)}, u32[]{:S(2)}) copy-start(f32[2,256,256]{2,1,0:T(8,128)S(1)} %get-tuple-element.569) | copy-start | bytes 1572868
  218.8 354.9 %collective-permute-start.2 = (f32[4,512,256]{2,1,0:T(8,128)S(1)}, f32[4,512,256]{2,1,0:T(8,128)S(1)}, u32[]{:S(2)}, u32[]{:S(2)}) collective-permute-start(f32[4,512,256]{2,1,0:T(8,128)S(1)} %slice.88), channel_id=1, source_target_pairs={{0,1},{1,2},{2,3},{3,4},{4,5},{5,6},{6,7},{8,9},{9,10},{10,11},{11... | collective-permute-start | bytes 6291464 | tf_op jit(solution)/shard_map/ppermute | solution.py:12
  575.6 1.9 copy-start.2
  579.0 31.9 %collective-permute-start.3 = (f32[4,256,512]{2,1,0:T(8,128)}, f32[4,256,512]{2,1,0:T(8,128)S(1)}, u32[]{:S(2)}, u32[]{:S(2)}) collective-permute-start(f32[4,256,512]{2,1,0:T(8,128)} %slice.98), channel_id=1, source_target_pairs={{0,8},{8,16},{16,24},{24,32},{32,40},{40,48},{48,56},{56,64},{64,7... | collective-permute-start | bytes 6291464 | tf_op jit(solution)/shard_map/ppermute | solution.py:12
Sparse Core Ops, SparseCore 0:
  581.2 176.1 all-reduce.1
where the time goes:
time: 770 us; the launch traced here: 766 us
  starting transfers between devices  360 us (47%)
  waiting for transfers between devices  233 us (30%)
  matrix products  66.9 us (9%)
  local copies, waits for them, and re-layouts  47.2 us (6%)
  other arithmetic  28.7 us (4%)
  loops' own time  16.2 us (2%)
  between operations  14.5 us (2%)
    ppermute x4, starting transfers between devices, from_behind(): lax.ppermute(value, axis, [(source, source + steps) for source in range(f...  360 us
    psum x1, waiting for transfers between devices, body(): probe_grad = lax.psum(probe_acc, ('row', 'col'))  143 us
    ppermute x4, waiting for transfers between devices, from_behind(): lax.ppermute(value, axis, [(source, source + steps) for source in range(f...  90 us
    dot_general x96, matrix products, real_dot(): jnp.dot(left, right, precision=lax.Precision.HIGHEST, preferred_element_t...  66.9 us
    dynamic_update_slice x2, local copies, waits for them, and re-layouts, add_window(): return lax.dynamic_update_slice(grad_ext, current + piece, start)  24.2 us
  transfers between devices with their start and end apart: 5, of which 5 were waited for; matrix products, arithmetic and copies ran while one was open for 1% of the time, Pallas kernels for 0%

commit v1 on v0

v1 whole, which is shorter than its diff:
```python
import math
import numpy as np
import ml_dtypes
import jax
import jax.numpy as jnp
from jax import lax
from jax.experimental import pallas as pl
from jax.experimental.pallas import tpu as pltpu
from jax.sharding import PartitionSpec as P

W = 256
F32 = jnp.float32
BF16 = jnp.bfloat16


def split_host(table):
    high = table.astype(np.float32).astype(ml_dtypes.bfloat16)
    low = (table - high.astype(np.float64)).astype(np.float32).astype(ml_dtypes.bfloat16)
    return high, low


def tables(width):
    index = np.arange(width)
    angles = 2.0 * np.pi / width * (index[:, None] * index[None, :] % width)
    dft = (np.cos(angles) - 1j * np.sin(angles)) / math.sqrt(width)
    freqs = np.where(index < width // 2, index, index - width) / width
    fresnel = np.exp(-1j * np.pi * (width / 4.0) * freqs**2)
    hop = np.conj(dft) @ (fresnel[:, None] * dft)
    out = []
    for table in (dft, hop):
        for part in (table.real, table.imag, -table.imag):
            out.extend(split_host(part))
    return np.stack(out)


def split(x):
    high = x.astype(BF16)
    return high, (x - high.astype(F32)).astype(BF16)


def kernel(meta, own, right, down0, down1, corner, amp, probe, tab,
           gown, gright, gdown0, gdown1, gcorner, gprobe,
           ext, gext, probe2, win, hs, zs, prop, xs, sems):
    width = W
    copies = [
        pltpu.make_async_copy(own, ext.at[0, :, :, pl.ds(0, 512)], sems.at[0]),
        pltpu.make_async_copy(right, ext.at[0, :, :, pl.ds(512, 256)], sems.at[1]),
        pltpu.make_async_copy(down0, ext.at[1, :, :, pl.ds(0, 256)], sems.at[2]),
        pltpu.make_async_copy(down1, ext.at[1, :, :, pl.ds(256, 256)], sems.at[3]),
        pltpu.make_async_copy(corner, ext.at[1, :, :, pl.ds(512, 256)], sems.at[4]),
    ]
    for copy in copies:
        copy.start()
    gext[...] = jnp.zeros_like(gext)
    gprobe[...] = jnp.zeros_like(gprobe)
    for copy in copies:
        copy.wait()
    live = meta[0]

    def block(table, part, level):
        return tab[table * 6 + part * 2 + level]

    def right_mul(x_ref, table, sign, out_ref):
        rh, rl = x_ref[0, :, :width], x_ref[1, :, :width]
        ih, il = x_ref[0, :, width:], x_ref[1, :, width:]
        lhs = jnp.concatenate([rh, ih, rl, il, rh, ih], axis=1)
        im, nim = (1, 2) if sign > 0 else (2, 1)
        def col(a, b):
            return jnp.concatenate([block(table, a, 0), block(table, b, 0), block(table, a, 0), block(table, b, 0), block(table, a, 1), block(table, b, 1)], axis=0)
        out_ref[:, :width] = jnp.dot(lhs, col(0, nim), preferred_element_type=F32)
        out_ref[:, width:] = jnp.dot(lhs, col(im, 0), preferred_element_type=F32)

    def left_mul(x_ref, table, sign, out_ref):
        rh, rl = x_ref[0, :, :width], x_ref[1, :, :width]
        ih, il = x_ref[0, :, width:], x_ref[1, :, width:]
        rhs = jnp.concatenate([rh, ih, rl, il, rh, ih], axis=0)
        im, nim = (1, 2) if sign > 0 else (2, 1)
        def row(a, b):
            return jnp.concatenate([block(table, a, 0), block(table, b, 0), block(table, a, 0), block(table, b, 0), block(table, a, 1), block(table, b, 1)], axis=1)
        out_ref[:, :width] = jnp.dot(row(0, nim), rhs, preferred_element_type=F32)
        out_ref[:, width:] = jnp.dot(row(im, 0), rhs, preferred_element_type=F32)

    R = 32
    n_chunks = width // R

    def chunks(body):
        def step(i, _):
            body(pl.multiple_of(i * R, R))
            return 0
        lax.fori_loop(0, n_chunks, step, 0)

    def put_split(at, re, im):
        h, l = split(re)
        xs[0, pl.ds(at, R), :width] = h
        xs[1, pl.ds(at, R), :width] = l
        h, l = split(im)
        xs[0, pl.ds(at, R), width:] = h
        xs[1, pl.ds(at, R), width:] = l

    def resplit():
        def body(at):
            put_split(at, hs[pl.ds(at, R), :width], hs[pl.ds(at, R), width:])
        chunks(body)

    def visit(s, _):
        r = meta[1 + s]
        c = meta[9 + s]
        cb = c // width
        cc = c - cb * width
        c0 = pl.multiple_of(cb * width, width)
        c1 = pl.multiple_of(cb * width + width, width)
        probe2[0] = pltpu.roll(pltpu.roll(probe[0], cc, 1), r, 0)
        probe2[1] = pltpu.roll(pltpu.roll(probe[1], cc, 1), r, 0)
        cmask = lax.broadcasted_iota(jnp.int32, (R, width), 1) >= cc

        def load(at):
            rmask = lax.broadcasted_iota(jnp.int32, (R, width), 0) + at >= r
            planes = []
            for p in range(4):
                top = jnp.where(cmask, ext[0, p, pl.ds(at, R), pl.ds(c0, width)], ext[0, p, pl.ds(at, R), pl.ds(c1, width)])
                bot = jnp.where(cmask, ext[1, p, pl.ds(at, R), pl.ds(c0, width)], ext[1, p, pl.ds(at, R), pl.ds(c1, width)])
                planes.append(jnp.where(rmask, top, bot))
            for p in range(4):
                win[p, pl.ds(at, R), :] = planes[p]
            pr, pi = probe2[0, pl.ds(at, R), :], probe2[1, pl.ds(at, R), :]
            put_split(at, pr * planes[0] - pi * planes[1], pr * planes[1] + pi * planes[0])
        chunks(load)
        right_mul(xs, 1, 1, hs)
        resplit()
        left_mul(xs, 1, 1, prop)
        def times_two(at):
            pr, pi = prop[pl.ds(at, R), :width], prop[pl.ds(at, R), width:]
            o, q = win[2, pl.ds(at, R), :], win[3, pl.ds(at, R), :]
            put_split(at, pr * o - pi * q, pr * q + pi * o)
        chunks(times_two)
        left_mul(xs, 0, 1, hs)
        resplit()
        right_mul(xs, 0, 1, zs)
        def chi(at):
            fr, fi = zs[pl.ds(at, R), :width], zs[pl.ds(at, R), width:]
            a = amp[s, pl.ds(at, R), :]
            factor = 1.0 - a * lax.rsqrt(fr * fr + fi * fi + 1.0)
            put_split(at, factor * fr, factor * fi)
        chunks(chi)
        right_mul(xs, 0, -1, hs)
        resplit()
        left_mul(xs, 0, -1, zs)
        def back(at):
            gr, gi = zs[pl.ds(at, R), :width], zs[pl.ds(at, R), width:]
            o, q = win[2, pl.ds(at, R), :], win[3, pl.ds(at, R), :]
            put_split(at, o * gr + q * gi, o * gi - q * gr)
            pr, pi = prop[pl.ds(at, R), :width], prop[pl.ds(at, R), width:]
            win[2, pl.ds(at, R), :] = pr * gr + pi * gi
            win[3, pl.ds(at, R), :] = pr * gi - pi * gr
        chunks(back)
        left_mul(xs, 1, -1, hs)
        resplit()
        right_mul(xs, 1, -1, zs)
        def finish(at):
            gr, gi = zs[pl.ds(at, R), :width], zs[pl.ds(at, R), width:]
            o, q = win[0, pl.ds(at, R), :], win[1, pl.ds(at, R), :]
            pr, pi = probe2[0, pl.ds(at, R), :], probe2[1, pl.ds(at, R), :]
            probe2[0, pl.ds(at, R), :] = o * gr + q * gi
            probe2[1, pl.ds(at, R), :] = o * gi - q * gr
            rmask = lax.broadcasted_iota(jnp.int32, (R, width), 0) + at >= r
            parts = [pr * gr + pi * gi, pr * gi - pi * gr, win[2, pl.ds(at, R), :], win[3, pl.ds(at, R), :]]
            zero = jnp.zeros((R, width), F32)
            for p in range(4):
                top = jnp.where(rmask, parts[p], zero)
                bot = jnp.where(rmask, zero, parts[p])
                for row, v in ((0, top), (1, bot)):
                    gext[row, p, pl.ds(at, R), pl.ds(c0, width)] += jnp.where(cmask, v, zero)
                    gext[row, p, pl.ds(at, R), pl.ds(c1, width)] += jnp.where(cmask, zero, v)
        chunks(finish)
        for p in range(2):
            gprobe[p] += pltpu.roll(pltpu.roll(probe2[p], width - cc, 1), width - r, 0)
        return 0

    lax.fori_loop(0, live, visit, 0)
    outs = [
        pltpu.make_async_copy(gext.at[0, :, :, pl.ds(0, 512)], gown, sems.at[0]),
        pltpu.make_async_copy(gext.at[0, :, :, pl.ds(512, 256)], gright, sems.at[1]),
        pltpu.make_async_copy(gext.at[1, :, :, pl.ds(0, 256)], gdown0, sems.at[2]),
        pltpu.make_async_copy(gext.at[1, :, :, pl.ds(256, 256)], gdown1, sems.at[3]),
        pltpu.make_async_copy(gext.at[1, :, :, pl.ds(512, 256)], gcorner, sems.at[4]),
    ]
    for copy in outs:
        copy.start()
    for copy in outs:
        copy.wait()


def slots_call(meta, own, right, down0, down1, corner, amp, probe, tab):
    any_spec = pl.BlockSpec(memory_space=pl.ANY)
    vmem = pl.BlockSpec(memory_space=pltpu.VMEM)
    shape = lambda *s: jax.ShapeDtypeStruct(s, F32)
    return pl.pallas_call(
        kernel,
        in_specs=[pl.BlockSpec(memory_space=pltpu.SMEM)] + [any_spec] * 5 + [vmem] * 3,
        out_specs=[any_spec] * 5 + [vmem],
        out_shape=[shape(4, 256, 512)] + [shape(4, 256, 256)] * 4 + [shape(2, 256, 256)],
        scratch_shapes=[
            pltpu.VMEM((2, 4, 256, 768), F32),
            pltpu.VMEM((2, 4, 256, 768), F32),
            pltpu.VMEM((2, 256, 256), F32),
            pltpu.VMEM((4, 256, 256), F32),
            pltpu.VMEM((256, 512), F32),
            pltpu.VMEM((256, 512), F32),
            pltpu.VMEM((256, 512), F32),
            pltpu.VMEM((2, 256, 512), BF16),
            pltpu.SemaphoreType.DMA((5,)),
        ],
        compiler_params=pltpu.CompilerParams(vmem_limit_bytes=50 * 2**20),
        cost_estimate=pl.CostEstimate(flops=8 * 100 * 2**25, bytes_accessed=20 * 2**20, transcendentals=0),
    )(meta, own, right, down0, down1, corner, amp, probe, tab)


def shift(value, axis, steps):
    count = lax.axis_size(axis)
    first, last = (max(0, -steps), min(count, count - steps))
    return lax.ppermute(value, axis, [(source, source + steps) for source in range(first, last)])


def sum_all(value, axes):
    count = lax.axis_size(axes)
    shares = value.reshape(count, -1, value.shape[-1])
    mine = lax.all_to_all(shares, axes, 0, 0, tiled=True).sum(axis=0)
    spread = jnp.broadcast_to(mine[None], shares.shape)
    return lax.all_to_all(spread, axes, 0, 0, tiled=True).reshape(value.shape)


def body(object_slab, probe_wave, scan_offsets, live_counts, amplitudes):
    rows_tile, cols_tile = object_slab.shape[1:]
    local_rows = scan_offsets[:, 0] - lax.axis_index("row") * rows_tile
    local_cols = scan_offsets[:, 1] - lax.axis_index("col") * cols_tile
    meta = jnp.concatenate([live_counts, local_rows, local_cols])
    first_half = object_slab[:, :, :W]
    down0 = shift(first_half, "row", -1)
    right = shift(first_half, "col", -1)
    down1 = shift(object_slab[:, :, W:], "row", -1)
    corner = shift(down0, "col", -1)
    tab = jnp.asarray(tables(W))
    gown, gright, gdown0, gdown1, gcorner, gprobe = slots_call(
        meta, object_slab, right, down0, down1, corner, amplitudes, probe_wave, tab
    )
    corner_back = shift(gcorner, "col", 1)
    down1_back = shift(gdown1, "row", 1)
    right_back = shift(gright, "col", 1)
    down0_back = shift(gdown0 + corner_back, "row", 1)
    probe_grad = sum_all(gprobe, ("row", "col"))
    object_grad = gown + jnp.concatenate([right_back + down0_back, down1_back], axis=2)
    return object_grad, probe_grad


def solution(mesh):
    return jax.shard_map(
        body,
        mesh=mesh,
        in_specs=(
            P(None, "row", "col"),
            P(),
            P(("row", "col"), None),
            P(("row", "col")),
            P(("row", "col"), None, None),
        ),
        out_specs=(P(None, "row", "col"), P()),
        check_vma=False,
    )
```

time: 770 us -> 215 us (0.28)
  starting transfers between devices: 360 us -> 19.4 us
  waiting for transfers between devices: 233 us -> 39.9 us
  blocking collectives: 0 us -> 77.1 us
  matrix products: 66.9 us -> 0 us
  Pallas kernels: 0 us -> 65.1 us
  local copies, waits for them, and re-layouts: 47.2 us -> 3.4 us
  other arithmetic: 28.7 us -> 5.83 us
  loops' own time: 16.2 us -> 0 us
  between operations: 14.5 us -> 1.43 us
    ppermute x4 -> x8, starting transfers between devices: 360 us -> 19.4 us  [shift(): lax.ppermute(value, axis, [(source, source + steps) for source in range(f...]
    psum x1 -> x0, waiting for transfers between devices: 143 us -> none  [body(): probe_grad = lax.psum(probe_acc, ('row', 'col'))]
    all_to_all x0 -> x2, blocking collectives: none -> 77.1 us  [the longest x1 58.3 us: sum_all(): mine = lax.all_to_all(shares, axes, 0, 0, tiled=True).sum(axis=0)]
    dot_general x96 -> x0, matrix products: 66.9 us -> none  [real_dot(): jnp.dot(left, right, precision=lax.Precision.HIGHEST, preferred_element_t...]
    pallas_call x0 -> x1, Pallas kernels: none -> 65.1 us  [slots_call(): pl.pallas_call(kernel, in_specs=[pl.BlockSpec(memory_space=pltpu.SMEM)] +...]
    ppermute x4 -> x8, waiting for transfers between devices: 90 us -> 39.9 us  [shift(): lax.ppermute(value, axis, [(source, source + steps) for source in range(f...]
    dynamic_update_slice x2 -> x0, local copies, waits for them, and re-layouts: 24.2 us -> none  [add_window(): return lax.dynamic_update_slice(grad_ext, current + piece, start)]
    another operation x9 -> x0, loops' own time: 16.2 us -> none  [the longest x8 8.22 us: visit(): return lax.cond(slot < live_count, active, lambda state: state, carry)]
  transfers between devices with their start and end apart: 5 -> 8, of which waited for: 5 -> 3; matrix products, arithmetic and copies ran while one was open for 1% -> 2% of each run, Pallas kernels for 0% -> 0%
where the time goes in v1:
time: 215 us; the launch traced here: 212 us
  blocking collectives  77.1 us (36%)
  Pallas kernels  65.1 us (30%)
  waiting for transfers between devices  39.9 us (19%)
  starting transfers between devices  19.4 us (9%)
  other arithmetic  5.83 us (3%)
  local copies, waits for them, and re-layouts  3.4 us (2%)
    pallas_call x1, Pallas kernels, slots_call(): pl.pallas_call(kernel, in_specs=[pl.BlockSpec(memory_space=pltpu.SMEM)] +...  65.1 us
    all_to_all x1, blocking collectives, sum_all(): mine = lax.all_to_all(shares, axes, 0, 0, tiled=True).sum(axis=0)  58.3 us
    ppermute x8, waiting for transfers between devices, shift(): lax.ppermute(value, axis, [(source, source + steps) for source in range(f...  39.9 us
    ppermute x8, starting transfers between devices, shift(): lax.ppermute(value, axis, [(source, source + steps) for source in range(f...  19.4 us
    all_to_all x1, blocking collectives, sum_all(): return lax.all_to_all(spread, axes, 0, 0, tiled=True).reshape(value.shape)  18.8 us
  transfers between devices with their start and end apart: 8, of which 3 were waited for; matrix products, arithmetic and copies ran while one was open for 2% of the time, Pallas kernels for 0%

profile of v1, /device:TPU:6, one launch (start us, length us, event | category | flops | bytes accessed | tf_op | source)
XLA Modules:
  0.0 212.1 jit_solution(7419815915677895916)
XLA Ops:
  0.6 0.0 copy-start.2
  0.6 0.0 copy-start
  0.6 1.8 fusion
  2.5 5.2 %collective-permute-start.1 = (f32[4,256,256]{2,1,0:T(8,128)S(1)}, f32[4,256,256]{2,1,0:T(8,128)}, u32[]{:S(2)}, u32[]{:S(2)}) collective-permute-start(f32[4,256,256]{2,1,0:T(8,128)S(1)} %get-tuple-element.15), channel_id=1, source_target_pairs={{8,0},{16,8},{24,16},{32,24},{40,32},{48,40},{56,48},{64,56},{72,6... | collective-permute-start | bytes 3145736 | tf_op jit(solution)/shard_map/ppermute | solution.py:221
  7.7 1.3 collective-permute-start
  9.0 2.7 %collective-permute-start.2 = (f32[4,256,256]{2,1,0:T(8,128)S(1)}, f32[4,256,256]{2,1,0:T(8,128)}, u32[]{:S(2)}, u32[]{:S(2)}) collective-permute-start(f32[4,256,256]{2,1,0:T(8,128)S(1)} %get-tuple-element.14), channel_id=1, source_target_pairs={{8,0},{16,8},{24,16},{32,24},{40,32},{48,40},{56,48},{64,56},{72,6... | collective-permute-start | bytes 3145736 | tf_op jit(solution)/shard_map/ppermute | solution.py:221
  11.6 19.6 %collective-permute-done.1.down0 = f32[4,256,256]{2,1,0:T(8,128)} collective-permute-done((f32[4,256,256]{2,1,0:T(8,128)S(1)}, f32[4,256,256]{2,1,0:T(8,128)}, u32[]{:S(2)}, u32[]{:S(2)}) %collective-permute-start.1) | collective-permute-done | bytes 1048608 | tf_op jit(solution)/shard_map/ppermute | solution.py:221
  31.2 1.3 collective-permute-start.3
  33.2 0.0 copy-done.2
  33.2 0.1 pad_add_fusion.meta
  33.3 19.3 %collective-permute-done.2.down1 = f32[4,256,256]{2,1,0:T(8,128)} collective-permute-done((f32[4,256,256]{2,1,0:T(8,128)S(1)}, f32[4,256,256]{2,1,0:T(8,128)}, u32[]{:S(2)}, u32[]{:S(2)}) %collective-permute-start.2) | collective-permute-done | bytes 1048608 | tf_op jit(solution)/shard_map/ppermute | solution.py:221
  52.5 0.0 collective-permute-done.right
  52.5 0.0 collective-permute-done.3.corner
  52.5 0.0 copy-done
  52.6 65.1 %shard_map.77 = (f32[4,256,512]{2,1,0:T(8,128)}, f32[4,256,256]{2,1,0:T(8,128)S(1)}, f32[4,256,256]{2,1,0:T(8,128)S(1)}, f32[4,256,256]{2,1,0:T(8,128)}, f32[4,2...) custom-call(s32[17]{0:T(128)S(1)} %pad_add_fusion.meta, f32[4,256,512]{2,1,0:T(8,128)} %own.1, ...), custom_call_target="tpu_custom_call" | custom-call | flops 26843545600 | bytes 20971520 | tf_op jit(solution)/shard_map/pallas_call | solution.py:197
  117.6 1.4 collective-permute-start.5
  119.0 1.4 collective-permute-start.4
  120.4 1.0 collective-permute-done.5
  121.4 1.1 add.9
  122.5 2.8 %collective-permute-start.6 = (f32[4,256,256]{2,1,0:T(8,128)}, f32[4,256,256]{2,1,0:T(8,128)}, u32[]{:S(2)}, u32[]{:S(2)}) collective-permute-start(f32[4,256,256]{2,1,0:T(8,128)} %add.9), channel_id=1, source_target_pairs={{0,8},{8,16},{16,24},{24,32},{32,40},{40,48},{48,56},{56,64},{64,7... | collective-permute-start | bytes 3145736 | tf_op jit(solution)/shard_map/ppermute | solution.py:221
  125.3 3.5 %collective-permute-start.7 = (f32[4,256,256]{2,1,0:T(8,128)}, f32[4,256,256]{2,1,0:T(8,128)}, u32[]{:S(2)}, u32[]{:S(2)}) collective-permute-start(f32[4,256,256]{2,1,0:T(8,128)} %get-tuple-element.12), channel_id=1, source_target_pairs={{0,8},{8,16},{16,24},{24,32},{32,40},{40,48},{48,56},{56,64},{64,7... | collective-permute-start | bytes 3145736 | tf_op jit(solution)/shard_map/ppermute | solution.py:221
  128.8 0.1 reshape.15
  128.9 58.3 %all_to_all.10 = f32[128,4,256]{2,1,0:T(4,128)S(1)} all-to-all(f32[128,4,256]{2,1,0:T(4,128)S(1)} %reshape.15), channel_id=1, replica_groups=mesh['row'=16,'col'=8] {'row','col'}, dimensions={0} | all-to-all | bytes 1048576 | tf_op jit(solution)/shard_map/all_to_all | solution.py:227
  187.2 0.1 reduce_sum.9
  187.4 0.1 broadcast_in_dim.2
  187.4 18.8 %all_to_all.11 = f32[128,4,256]{2,1,0:T(4,128)S(1)} all-to-all(f32[128,4,256]{2,1,0:T(4,128)S(1)} %broadcast_in_dim.2), channel_id=1, replica_groups=mesh['row'=16,'col'=8] {'row','col'}, dimensions={0} | all-to-all | bytes 1048576 | tf_op jit(solution)/shard_map/all_to_all | solution.py:229
  206.3 1.0 reshape.16
  207.2 0.0 copy-start.1
  207.2 0.0 collective-permute-done.4
  207.3 0.0 collective-permute-done.6
  207.3 1.5 add.10
  208.8 0.0 collective-permute-done.7
  208.8 0.4 copy-done.1
  209.2 3.0 %maximum_add_fusion = f32[4,256,512]{2,1,0:T(8,128)} fusion(f32[4,256,512]{2,1,0:T(8,128)S(1)} %copy-done.1, f32[4,256,256]{2,1,0:T(8,128)} %collective-permute-done.7, f32[4,256,256]{2,1,0:T(8,128)S(1)} %add.10), kind=kLoop, calls=%fused_computation | loop fusion | flops 1048576 | bytes 6291456 | tf_op jit(solution)/shard_map/add | solution.py:251
  (1 shorter events, 0.0 us)
Async XLA Ops:
  0.6 32.5 %copy-start.2 = (s32[8,2]{0,1:T(2,128)S(1)}, s32[8,2]{0,1:T(2,128)}, u32[]{:S(2)}) copy-start(s32[8,2]{0,1:T(2,128)} %param.8) | copy-start | bytes 196
  0.6 51.9 %copy-start = (f32[2,256,256]{2,1,0:T(8,128)S(1)}, f32[2,256,256]{2,1,0:T(8,128)}, u32[]{:S(2)}) copy-start(f32[2,256,256]{2,1,0:T(8,128)} %probe.1) | copy-start | bytes 1572868
  2.5 28.7 %collective-permute-start.1 = (f32[4,256,256]{2,1,0:T(8,128)S(1)}, f32[4,256,256]{2,1,0:T(8,128)}, u32[]{:S(2)}, u32[]{:S(2)}) collective-permute-start(f32[4,256,256]{2,1,0:T(8,128)S(1)} %get-tuple-element.15), channel_id=1, source_target_pairs={{8,0},{16,8},{24,16},{32,24},{40,32},{48,40},{56,48},{64,56},{72,6... | collective-permute-start | bytes 3145736 | tf_op jit(solution)/shard_map/ppermute | solution.py:221
  7.7 44.9 %collective-permute-start = (f32[4,256,256]{2,1,0:T(8,128)S(1)}, f32[4,256,256]{2,1,0:T(8,128)}, u32[]{:S(2)}, u32[]{:S(2)}) collective-permute-start(f32[4,256,256]{2,1,0:T(8,128)S(1)} %get-tuple-element.15), channel_id=1, source_target_pairs={{1,0},{2,1},{3,2},{4,3},{5,4},{6,5},{7,6},{9,8},{10,9},{11,10},{12... | collective-permute-start | bytes 3145736 | tf_op jit(solution)/shard_map/ppermute | solution.py:221
  9.0 43.6 %collective-permute-start.2 = (f32[4,256,256]{2,1,0:T(8,128)S(1)}, f32[4,256,256]{2,1,0:T(8,128)}, u32[]{:S(2)}, u32[]{:S(2)}) collective-permute-start(f32[4,256,256]{2,1,0:T(8,128)S(1)} %get-tuple-element.14), channel_id=1, source_target_pairs={{8,0},{16,8},{24,16},{32,24},{40,32},{48,40},{56,48},{64,56},{72,6... | collective-permute-start | bytes 3145736 | tf_op jit(solution)/shard_map/ppermute | solution.py:221
  31.2 21.3 %collective-permute-start.3 = (f32[4,256,256]{2,1,0:T(8,128)}, f32[4,256,256]{2,1,0:T(8,128)}, u32[]{:S(2)}, u32[]{:S(2)}) collective-permute-start(f32[4,256,256]{2,1,0:T(8,128)} %collective-permute-done.1.down0), channel_id=1, source_target_pairs={{1,0},{2,1},{3,2},{4,3},{5,4},{6,5},{7,6},{9,8},{10,9},{11,10},{12... | collective-permute-start | bytes 3145736 | tf_op jit(solution)/shard_map/ppermute | solution.py:221
  117.6 3.8 %collective-permute-start.5 = (f32[4,256,256]{2,1,0:T(8,128)}, f32[4,256,256]{2,1,0:T(8,128)S(1)}, u32[]{:S(2)}, u32[]{:S(2)}) collective-permute-start(f32[4,256,256]{2,1,0:T(8,128)} %get-tuple-element.11), channel_id=1, source_target_pairs={{0,1},{1,2},{2,3},{3,4},{4,5},{5,6},{6,7},{8,9},{9,10},{10,11},{11... | collective-permute-start | bytes 3145736 | tf_op jit(solution)/shard_map/ppermute | solution.py:221
  119.0 88.3 %collective-permute-start.4 = (f32[4,256,256]{2,1,0:T(8,128)S(1)}, f32[4,256,256]{2,1,0:T(8,128)S(1)}, u32[]{:S(2)}, u32[]{:S(2)}) collective-permute-start(f32[4,256,256]{2,1,0:T(8,128)S(1)} %get-tuple-element.9), channel_id=1, source_target_pairs={{0,1},{1,2},{2,3},{3,4},{4,5},{5,6},{6,7},{8,9},{9,10},{10,11},{11... | collective-permute-start | bytes 3145736 | tf_op jit(solution)/shard_map/ppermute | solution.py:221
  122.5 84.7 %collective-permute-start.6 = (f32[4,256,256]{2,1,0:T(8,128)}, f32[4,256,256]{2,1,0:T(8,128)}, u32[]{:S(2)}, u32[]{:S(2)}) collective-permute-start(f32[4,256,256]{2,1,0:T(8,128)} %add.9), channel_id=1, source_target_pairs={{0,8},{8,16},{16,24},{24,32},{32,40},{40,48},{48,56},{56,64},{64,7... | collective-permute-start | bytes 3145736 | tf_op jit(solution)/shard_map/ppermute | solution.py:221
  125.3 83.5 %collective-permute-start.7 = (f32[4,256,256]{2,1,0:T(8,128)}, f32[4,256,256]{2,1,0:T(8,128)}, u32[]{:S(2)}, u32[]{:S(2)}) collective-permute-start(f32[4,256,256]{2,1,0:T(8,128)} %get-tuple-element.12), channel_id=1, source_target_pairs={{0,8},{8,16},{16,24},{24,32},{32,40},{40,48},{48,56},{56,64},{64,7... | collective-permute-start | bytes 3145736 | tf_op jit(solution)/shard_map/ppermute | solution.py:221
  207.2 1.9 copy-start.1

commit v2 on v0

v2 whole, which is shorter than its diff:
```python
import math

import jax
import jax.numpy as jnp
import ml_dtypes
import numpy as np
from jax import lax
from jax.experimental import pallas as pl
from jax.experimental.pallas import tpu as pltpu
from jax.sharding import PartitionSpec as P

W = 256
HALF_W = 128
TC = 512
EXT = TC + W
SLOTS = 8
GROUP = 4
CHUNK = 32
F32 = jnp.float32
BF16 = jnp.bfloat16

RE, IM, NEG_IM = 0, 1, 2


def split_host(table):
    high = table.astype(np.float32).astype(ml_dtypes.bfloat16)
    low = (table - high.astype(np.float64)).astype(np.float32).astype(ml_dtypes.bfloat16)
    return [high, low]


def hop_tables():
    index = np.arange(W)
    dft = np.exp(-2j * np.pi / W * (index[:, None] * index[None, :] % W)) / math.sqrt(W)
    freqs = np.where(index < W // 2, index, index - W) / W
    fresnel = np.exp(-1j * np.pi * (W / 4.0) * freqs**2)
    hop = np.conj(dft) @ (fresnel[:, None] * dft)
    hop = hop * np.exp(1j * np.pi * index / W)
    out = []
    for table in (hop, hop.T):
        for part in (table.real, table.imag, -table.imag):
            out.extend(split_host(part))
    return np.stack(out)


def dft_tables():
    index = np.arange(W)
    angles = 2.0 * np.pi / W * (index[:, None] + 0.5) * (index[None, :HALF_W] + 0.5)
    table = np.concatenate([np.cos(angles), np.sin(angles)], axis=1) / math.sqrt(W)
    return np.stack(split_host(table) + split_host(table.T))


def fold_tables():
    source = np.concatenate([np.arange(HALF_W), np.arange(W - 1, HALF_W - 1, -1)])
    table = np.zeros((W, W), np.float32)
    table[source, np.arange(W)] = 1.0
    return np.stack([table, table.T]).astype(ml_dtypes.bfloat16)


def split(x):
    high = x.astype(BF16)
    return high, (x - high.astype(F32)).astype(BF16)


def lanes(*parts):
    return jnp.concatenate(parts, axis=1)


def rows(*parts):
    return jnp.concatenate(parts, axis=0)


def dot(a, b):
    return jnp.dot(a, b, preferred_element_type=F32)


def half_right(field, tab, at):
    high, low = tab[2 * at], tab[2 * at + 1]
    rh, rl = split(field[0])
    ih, il = split(field[1])
    out = dot(rows(lanes(rh, rl, rh), lanes(ih, il, ih)), rows(high, high, low))
    return out[:W], out[W:]


def half_left(field, tab, at):
    high, low = tab[2 * at], tab[2 * at + 1]
    rh, rl = split(field[0])
    ih, il = split(field[1])
    out = dot(lanes(high, high, low), lanes(rows(rh, rl, rh), rows(ih, il, ih)))
    return out[:, :W], out[:, W:]


def hop_parts(tab, at, conj):
    im, neg = (IM, NEG_IM) if not conj else (NEG_IM, IM)

    def three(a, b):
        a, b = 2 * (3 * at + a), 2 * (3 * at + b)
        return [tab[a], tab[b], tab[a], tab[b], tab[a + 1], tab[b + 1]]

    return three(RE, neg), three(im, RE)


def hop_right(field, tab, at, conj):
    rh, rl = split(field[0])
    ih, il = split(field[1])
    to_re, to_im = hop_parts(tab, at, conj)
    out = dot(lanes(rh, ih, rl, il, rh, ih), lanes(rows(*to_re), rows(*to_im)))
    return out[:, :W], out[:, W:]


def hop_left(field, tab, at, conj):
    rh, rl = split(field[0])
    ih, il = split(field[1])
    to_re, to_im = hop_parts(tab, at, conj)
    out = dot(rows(lanes(*to_re), lanes(*to_im)), rows(rh, ih, rl, il, rh, ih))
    return out[:W], out[W:]


def spread_right(field):
    c, s = field[0][:, :HALF_W], field[0][:, HALF_W:]
    d, t = field[1][:, :HALF_W], field[1][:, HALF_W:]
    return lanes(c + t, t - c), lanes(d - s, -d - s)


def spread_left(field):
    c, s = field[0][:HALF_W], field[0][HALF_W:]
    d, t = field[1][:HALF_W], field[1][HALF_W:]
    return rows(c + t, t - c), rows(d - s, -d - s)


def gather_right(field):
    a, b = field[0][:, :HALF_W], field[0][:, HALF_W:]
    c, d = field[1][:, :HALF_W], field[1][:, HALF_W:]
    return lanes(a - b, -c - d), lanes(c - d, a + b)


def gather_left(field):
    a, b = field[0][:HALF_W], field[0][HALF_W:]
    c, d = field[1][:HALF_W], field[1][HALF_W:]
    return rows(a - b, -c - d), rows(c - d, a + b)


def times(a, b):
    return a[0] * b[0] - a[1] * b[1], a[0] * b[1] + a[1] * b[0]


def conj_times(a, b):
    return a[0] * b[0] + a[1] * b[1], a[0] * b[1] - a[1] * b[0]


def pair(ref, *at):
    return ref[(*at, 0)], ref[(*at, 1)]


def put(value, ref, *at):
    ref[(*at, 0)], ref[(*at, 1)] = value


def chunks(body):
    def step(i, carry):
        body(pl.multiple_of(i * CHUNK, CHUNK))
        return carry

    lax.fori_loop(0, W // CHUNK, step, 0)


def geometry(meta, slot):
    row, col = meta[1 + slot], meta[1 + SLOTS + slot]
    block = col // W
    first = pl.multiple_of(block * W, W)
    second = pl.multiple_of(block * W + W, W)
    return row, col - block * W, first, second


def masks(row, col, at):
    in_top = lax.broadcasted_iota(jnp.int32, (CHUNK, W), 0) + at >= row
    in_first = lax.broadcasted_iota(jnp.int32, (CHUNK, W), 1) >= col
    return in_top, in_first


def load_window(meta, slot, ext, win, u):
    row, col, first, second = geometry(meta, slot)

    def load(at):
        in_top, in_first = masks(row, col, at)
        here = pl.ds(at, CHUNK)
        for p in range(2):
            top = jnp.where(in_first, ext[0, p, here, pl.ds(first, W)], ext[0, p, here, pl.ds(second, W)])
            low = jnp.where(in_first, ext[1, p, here, pl.ds(first, W)], ext[1, p, here, pl.ds(second, W)])
            win[u, p, here, :] = jnp.where(in_top, top, low)

    chunks(load)


def add_window(meta, slot, win, u, gext):
    row, col, first, second = geometry(meta, slot)

    def add(at):
        in_top, in_first = masks(row, col, at)
        here = pl.ds(at, CHUNK)
        zero = jnp.zeros((CHUNK, W), F32)
        for p in range(2):
            value = win[u, p, here, :]
            for r, part in ((0, jnp.where(in_top, value, zero)), (1, jnp.where(in_top, zero, value))):
                gext[r, p, here, pl.ds(first, W)] += jnp.where(in_first, part, zero)
                gext[r, p, here, pl.ds(second, W)] += jnp.where(in_first, zero, part)

    chunks(add)


def turn(plane, row, col):
    return pltpu.roll(pltpu.roll(plane, col, 1), row, 0)


def tile_copies(planes, refs, ext, sems, out):
    own, right, down0, down1, corner = refs
    inner = [
        (own if planes is None else own.at[planes], ext.at[0, :, :, pl.ds(0, TC)]),
        (right, ext.at[0, :, :, pl.ds(TC, W)]),
        (down0, ext.at[1, :, :, pl.ds(0, W)]),
        (down1, ext.at[1, :, :, pl.ds(W, W)]),
        (corner, ext.at[1, :, :, pl.ds(TC, W)]),
    ]
    return [
        pltpu.make_async_copy(*((b, a) if out else (a, b)), sems.at[i])
        for i, (a, b) in enumerate(inner)
    ]


def run_copies(copies, between=None):
    for copy in copies:
        copy.start()
    if between is not None:
        between()
    for copy in copies:
        copy.wait()


def first_kernel(meta, own, right, down0, down1, corner, probe, amp, tab, fold, prop, amp_out, ext, turned, win, sems):
    step = pl.program_id(0)

    def fold_amplitudes(u):
        high = amp[u].astype(BF16)
        rest = amp[u] - high.astype(F32)
        mid = rest.astype(BF16)
        low = (rest - mid.astype(F32)).astype(BF16)
        right_way = dot(rows(high, mid, low), fold[0])
        out = dot(fold[1], lanes(*(right_way[i * W : (i + 1) * W].astype(BF16) for i in range(3))))
        amp_out[u] = out[:, :W] + out[:, W : 2 * W] + out[:, 2 * W :]

    pl.when(step == 0)(lambda: run_copies(tile_copies(pl.ds(0, 2), (own, right, down0, down1, corner), ext, sems, False)))

    @pl.when(step * GROUP < meta[0])
    def work():
        for u in range(GROUP):
            slot = step * GROUP + u
            load_window(meta, slot, ext, win, u)
            row, col, _, _ = geometry(meta, slot)
            for p in range(2):
                turned[u, p] = turn(probe[p], row, col)
        fields = [times(pair(turned, u), pair(win, u)) for u in range(GROUP)]
        fields = [hop_right(f, tab, 0, False) for f in fields]
        fields = [hop_left(f, tab, 1, False) for f in fields]
        for u, f in enumerate(fields):
            put(f, prop, u)
            fold_amplitudes(u)


def second_kernel(meta, own, right, down0, down1, corner, prop, amp, tab, gown, gright, gdown0, gdown1, gcorner, back, ext, gext, win, sems):
    step = pl.program_id(0)

    @pl.when(step == 0)
    def begin():
        def clear():
            gext[...] = jnp.zeros_like(gext)

        run_copies(tile_copies(pl.ds(2, 2), (own, right, down0, down1, corner), ext, sems, False), clear)

    @pl.when(step * GROUP < meta[0])
    def work():
        group = range(GROUP)
        for u in group:
            load_window(meta, step * GROUP + u, ext, win, u)
        fields = [times(pair(prop, u), pair(win, u)) for u in group]
        fields = [spread_left(half_left(f, tab, 1)) for f in fields]
        fields = [spread_right(half_right(f, tab, 0)) for f in fields]
        chi = []
        for u, f in enumerate(fields):
            factor = 1.0 - amp[u] * lax.rsqrt(f[0] * f[0] + f[1] * f[1] + 1.0)
            chi.append((factor * f[0], factor * f[1]))
        fields = [half_right(gather_right(f), tab, 1) for f in chi]
        fields = [half_left(gather_left(f), tab, 0) for f in fields]
        for u, f in enumerate(fields):
            put(conj_times(pair(win, u), f), back, u)
        for u, f in enumerate(fields):
            put(conj_times(pair(prop, u), f), win, u)
        for u in group:
            slot = step * GROUP + u
            pl.when(slot < meta[0])(lambda: add_window(meta, slot, win, u, gext))

    @pl.when(step == SLOTS // GROUP - 1)
    def end():
        run_copies(tile_copies(None, (gown, gright, gdown0, gdown1, gcorner), gext, sems, True))


def third_kernel(meta, own, right, down0, down1, corner, probe, back, tab, gown, gright, gdown0, gdown1, gcorner, gprobe, ext, gext, turned, win, sems):
    step = pl.program_id(0)

    @pl.when(step == 0)
    def begin():
        def clear():
            gext[...] = jnp.zeros_like(gext)
            gprobe[...] = jnp.zeros_like(gprobe)

        run_copies(tile_copies(pl.ds(0, 2), (own, right, down0, down1, corner), ext, sems, False), clear)

    @pl.when(step * GROUP < meta[0])
    def work():
        group = range(GROUP)
        for u in group:
            slot = step * GROUP + u
            load_window(meta, slot, ext, win, u)
            row, col, _, _ = geometry(meta, slot)
            for p in range(2):
                turned[u, p] = turn(probe[p], row, col)
        fields = [hop_left(pair(back, u), tab, 0, True) for u in group]
        fields = [hop_right(f, tab, 1, True) for f in fields]
        for u, f in enumerate(fields):
            grad, probe_part = conj_times(pair(turned, u), f), conj_times(pair(win, u), f)
            put(grad, win, u)
            put(probe_part, turned, u)

        def finish(slot, u):
            add_window(meta, slot, win, u, gext)
            row, col, _, _ = geometry(meta, slot)
            for p in range(2):
                gprobe[p] += turn(turned[u, p], W - row, W - col)

        for u in group:
            slot = step * GROUP + u
            pl.when(slot < meta[0])(lambda: finish(slot, u))

    @pl.when(step == SLOTS // GROUP - 1)
    def end():
        run_copies(tile_copies(None, (gown, gright, gdown0, gdown1, gcorner), gext, sems, True))


ANYWHERE = pl.BlockSpec(memory_space=pl.ANY)
WHOLE = pl.BlockSpec(memory_space=pltpu.VMEM)
SCALARS = pl.BlockSpec(memory_space=pltpu.SMEM)
FIELDS = pl.BlockSpec((GROUP, 2, W, W), lambda i: (i, 0, 0, 0))
PLANES = pl.BlockSpec((GROUP, W, W), lambda i: (i, 0, 0))


def shape(*dims):
    return jax.ShapeDtypeStruct(dims, F32)


FIELDS_SHAPE = shape(SLOTS, 2, W, W)
TILE_SHAPES = [shape(2, W, TC)] + [shape(2, W, W)] * 4
EXT_SCRATCH = pltpu.VMEM((2, 2, W, EXT), F32)
GROUP_SCRATCH = pltpu.VMEM((GROUP, 2, W, W), F32)
SEMS = pltpu.SemaphoreType.DMA((5,))


def call(kernel, in_specs, out_specs, out_shape, scratch, products):
    return pl.pallas_call(
        kernel,
        grid=(SLOTS // GROUP,),
        in_specs=in_specs,
        out_specs=out_specs,
        out_shape=out_shape,
        scratch_shapes=scratch,
        compiler_params=pltpu.CompilerParams(
            vmem_limit_bytes=56 * 2**20, dimension_semantics=("arbitrary",)
        ),
        cost_estimate=pl.CostEstimate(
            flops=SLOTS * products * 2 * W**3, bytes_accessed=12 * 2**20, transcendentals=0
        ),
    )


def first_call(*args):
    return call(
        first_kernel,
        [SCALARS] + [ANYWHERE] * 5 + [WHOLE, PLANES, WHOLE, WHOLE],
        [FIELDS, PLANES],
        [FIELDS_SHAPE, shape(SLOTS, W, W)],
        [EXT_SCRATCH, GROUP_SCRATCH, GROUP_SCRATCH, SEMS],
        24,
    )(*args)


def second_call(*args):
    return call(
        second_kernel,
        [SCALARS] + [ANYWHERE] * 5 + [FIELDS, PLANES, WHOLE],
        [ANYWHERE] * 5 + [FIELDS],
        TILE_SHAPES + [FIELDS_SHAPE],
        [EXT_SCRATCH, EXT_SCRATCH, GROUP_SCRATCH, SEMS],
        24,
    )(*args)


def third_call(*args):
    return call(
        third_kernel,
        [SCALARS] + [ANYWHERE] * 5 + [WHOLE, FIELDS, WHOLE],
        [ANYWHERE] * 5 + [WHOLE],
        TILE_SHAPES + [shape(2, W, W)],
        [EXT_SCRATCH, EXT_SCRATCH, GROUP_SCRATCH, GROUP_SCRATCH, SEMS],
        24,
    )(*args)


def shift(value, axis, steps):
    count = lax.axis_size(axis)
    first, last = (max(0, -steps), min(count, count - steps))
    return lax.ppermute(value, axis, [(source, source + steps) for source in range(first, last)])


def fetch(tile):
    first_half = tile[:, :, :W]
    down0 = shift(first_half, "row", -1)
    down1 = shift(tile[:, :, W:], "row", -1)
    right = shift(first_half, "col", -1)
    corner = shift(down0, "col", -1)
    return right, down0, down1, corner


def hand_back(gright, gdown0, gdown1, gcorner):
    corner_back = shift(gcorner, "col", 1)
    down1_back = shift(gdown1, "row", 1)
    right_back = shift(gright, "col", 1)
    down0_back = shift(gdown0 + corner_back, "row", 1)
    return jnp.concatenate([right_back + down0_back, down1_back], axis=2)


def sum_all(value, axes):
    count = lax.axis_size(axes)
    shares = value.reshape(count, -1, value.shape[-1])
    mine = lax.all_to_all(shares, axes, 0, 0, tiled=True).sum(axis=0)
    spread = jnp.broadcast_to(mine[None], shares.shape)
    return lax.all_to_all(spread, axes, 0, 0, tiled=True).reshape(value.shape)


def body(object_slab, probe_wave, scan_offsets, live_counts, amplitudes):
    rows_tile, cols_tile = object_slab.shape[1:]
    local_rows = scan_offsets[:, 0] - lax.axis_index("row") * rows_tile
    local_cols = scan_offsets[:, 1] - lax.axis_index("col") * cols_tile
    meta = jnp.concatenate([live_counts, local_rows, local_cols])
    hop, dft, fold = jnp.asarray(hop_tables()), jnp.asarray(dft_tables()), jnp.asarray(fold_tables())
    near_one = fetch(object_slab[:2])
    near_two = fetch(object_slab[2:])
    prop, amp = first_call(meta, object_slab, *near_one, probe_wave, amplitudes, hop, fold)
    *grads_two, back = second_call(meta, object_slab, *near_two, prop, amp, dft)
    *grads_one, gprobe = third_call(meta, object_slab, *near_one, probe_wave, back, hop)
    back_two = hand_back(*grads_two[1:])
    back_one = hand_back(*grads_one[1:])
    probe_grad = sum_all(gprobe, ("row", "col"))
    object_grad = jnp.concatenate([grads_one[0] + back_one, grads_two[0] + back_two], axis=0)
    return object_grad, probe_grad


def solution(mesh):
    return jax.shard_map(
        body,
        mesh=mesh,
        in_specs=(
            P(None, "row", "col"),
            P(),
            P(("row", "col"), None),
            P(("row", "col")),
            P(("row", "col"), None, None),
        ),
        out_specs=(P(None, "row", "col"), P()),
        check_vma=False,
    )
```

time: 770 us -> 197 us (0.26)
  starting transfers between devices: 360 us -> 87.5 us
  waiting for transfers between devices: 233 us -> 48.8 us
  matrix products: 66.9 us -> 0 us
  Pallas kernels: 0 us -> 40.4 us
  local copies, waits for them, and re-layouts: 47.2 us -> 7.31 us
  other arithmetic: 28.7 us -> 10.1 us
  loops' own time: 16.2 us -> 0 us
  between operations: 14.5 us -> 1.67 us
    ppermute x4 -> x16, starting transfers between devices: 360 us -> 46.3 us  [shift(): lax.ppermute(value, axis, [(source, source + steps) for source in range(f...]
    psum x1 -> x0, waiting for transfers between devices: 143 us -> none  [body(): probe_grad = lax.psum(probe_acc, ('row', 'col'))]
    ppermute x4 -> x16, waiting for transfers between devices: 90 us -> 21.4 us  [shift(): lax.ppermute(value, axis, [(source, source + steps) for source in range(f...]
    dot_general x96 -> x0, matrix products: 66.9 us -> none  [real_dot(): jnp.dot(left, right, precision=lax.Precision.HIGHEST, preferred_element_t...]
    all_to_all x0 -> x2, starting transfers between devices: none -> 41.2 us  [the longest x1 32.1 us: sum_all(): mine = lax.all_to_all(shares, axes, 0, 0, tiled=True).sum(axis=0)]
    pallas_call x0 -> x3, Pallas kernels: none -> 40.4 us  [the longest x1 14.2 us: third_call(): call(third_kernel, [SCALARS] + [ANYWHERE] * 5 + [WHOLE, FIELDS, WHOLE], [...]
    all_to_all x0 -> x2, waiting for transfers between devices: none -> 27.4 us  [the longest x1 27.4 us: sum_all(): return lax.all_to_all(spread, axes, 0, 0, tiled=True).reshape(value.shape)]
    dynamic_update_slice x2 -> x0, local copies, waits for them, and re-layouts: 24.2 us -> none  [add_window(): return lax.dynamic_update_slice(grad_ext, current + piece, start)]
  transfers between devices with their start and end apart: 5 -> 18, of which waited for: 5 -> 5; matrix products, arithmetic and copies ran while one was open for 1% -> 6% of each run, Pallas kernels for 0% -> 7%
where the time goes in v2:
time: 197 us; the launch traced here: 196 us
  starting transfers between devices  87.5 us (44%)
  waiting for transfers between devices  48.8 us (25%)
  Pallas kernels  40.4 us (21%)
  other arithmetic  10.1 us (5%)
  local copies, waits for them, and re-layouts  7.31 us (4%)
    ppermute x16, starting transfers between devices, shift(): lax.ppermute(value, axis, [(source, source + steps) for source in range(f...  46.3 us
    all_to_all x1, starting transfers between devices, sum_all(): mine = lax.all_to_all(shares, axes, 0, 0, tiled=True).sum(axis=0)  32.1 us
    all_to_all x1, waiting for transfers between devices, sum_all(): return lax.all_to_all(spread, axes, 0, 0, tiled=True).reshape(value.shape)  27.4 us
    ppermute x16, waiting for transfers between devices, shift(): lax.ppermute(value, axis, [(source, source + steps) for source in range(f...  21.4 us
    pallas_call x1, Pallas kernels, third_call(): call(third_kernel, [SCALARS] + [ANYWHERE] * 5 + [WHOLE, FIELDS, WHOLE], [...  14.2 us
    pallas_call x1, Pallas kernels, second_call(): call(second_kernel, [SCALARS] + [ANYWHERE] * 5 + [FIELDS, PLANES, WHOLE],...  13.4 us
    pallas_call x1, Pallas kernels, first_call(): call(first_kernel, [SCALARS] + [ANYWHERE] * 5 + [WHOLE, PLANES, WHOLE, WH...  12.8 us
    all_to_all x1, starting transfers between devices, sum_all(): return lax.all_to_all(spread, axes, 0, 0, tiled=True).reshape(value.shape)  9.06 us
  transfers between devices with their start and end apart: 18, of which 5 were waited for; matrix products, arithmetic and copies ran while one was open for 6% of the time, Pallas kernels for 7%

profile of v2, /device:TPU:6, one launch (start us, length us, event | category | flops | bytes accessed | tf_op | source)
XLA Modules:
  0.0 195.8 jit_solution(10626242851413282929)
XLA Ops:
  0.6 0.0 copy-start.5
  0.6 1.7 fusion
  2.3 5.2 %collective-permute-start.1 = (f32[2,256,256]{2,1,0:T(8,128)S(1)}, f32[2,256,256]{2,1,0:T(8,128)S(1)}, u32[]{:S(2)}, u32[]{:S(2)}) collective-permute-start(f32[2,256,256]{2,1,0:T(8,128)S(1)} %get-tuple-element.33), channel_id=1, source_target_pairs={{8,0},{16,8},{24,16},{32,24},{40,32},{48,40},{56,48},{64,56},{72,6... | collective-permute-start | bytes 1572872 | tf_op jit(solution)/shard_map/ppermute | solution.py:418
  7.5 2.7 %collective-permute-start.2 = (f32[2,256,256]{2,1,0:T(8,128)S(1)}, f32[2,256,256]{2,1,0:T(8,128)S(1)}, u32[]{:S(2)}, u32[]{:S(2)}) collective-permute-start(f32[2,256,256]{2,1,0:T(8,128)S(1)} %get-tuple-element.30), channel_id=1, source_target_pairs={{8,0},{16,8},{24,16},{32,24},{40,32},{48,40},{56,48},{64,56},{72,6... | collective-permute-start | bytes 1572872 | tf_op jit(solution)/shard_map/ppermute | solution.py:418
  10.2 2.4 %collective-permute-start.5 = (f32[2,256,256]{2,1,0:T(8,128)S(1)}, f32[2,256,256]{2,1,0:T(8,128)}, u32[]{:S(2)}, u32[]{:S(2)}) collective-permute-start(f32[2,256,256]{2,1,0:T(8,128)S(1)} %get-tuple-element.32), channel_id=1, source_target_pairs={{8,0},{16,8},{24,16},{32,24},{40,32},{48,40},{56,48},{64,56},{72,6... | collective-permute-start | bytes 1572872 | tf_op jit(solution)/shard_map/ppermute | solution.py:418
  12.5 1.3 collective-permute-start
  13.8 6.0 %collective-permute-done.1.down0 = f32[2,256,256]{2,1,0:T(8,128)S(1)} collective-permute-done((f32[2,256,256]{2,1,0:T(8,128)S(1)}, f32[2,256,256]{2,1,0:T(8,128)S(1)}, u32[]{:S(2)}, u32[]{:S(2)}) %collective-permute-start.1) | collective-permute-done | bytes 524320 | tf_op jit(solution)/shard_map/ppermute | solution.py:418
  19.8 1.3 collective-permute-start.3
  21.1 1.3 collective-permute-start.4
  23.0 0.0 copy-done.5
  23.1 0.7 pad_add_fusion.meta
  23.7 7.3 %collective-permute-done.2.down1 = f32[2,256,256]{2,1,0:T(8,128)S(1)} collective-permute-done((f32[2,256,256]{2,1,0:T(8,128)S(1)}, f32[2,256,256]{2,1,0:T(8,128)S(1)}, u32[]{:S(2)}, u32[]{:S(2)}) %collective-permute-start.2) | collective-permute-done | bytes 524320 | tf_op jit(solution)/shard_map/ppermute | solution.py:418
  31.0 6.5 %collective-permute-start.6 = (f32[2,256,256]{2,1,0:T(8,128)S(1)}, f32[2,256,256]{2,1,0:T(8,128)S(1)}, u32[]{:S(2)}, u32[]{:S(2)}) collective-permute-start(f32[2,256,256]{2,1,0:T(8,128)S(1)} %get-tuple-element.31), channel_id=1, source_target_pairs={{8,0},{16,8},{24,16},{32,24},{40,32},{48,40},{56,48},{64,56},{72,6... | collective-permute-start | bytes 1572872 | tf_op jit(solution)/shard_map/ppermute | solution.py:418
  37.5 4.7 %collective-permute-done.5.down0 = f32[2,256,256]{2,1,0:T(8,128)} collective-permute-done((f32[2,256,256]{2,1,0:T(8,128)S(1)}, f32[2,256,256]{2,1,0:T(8,128)}, u32[]{:S(2)}, u32[]{:S(2)}) %collective-permute-start.5) | collective-permute-done | bytes 524320 | tf_op jit(solution)/shard_map/ppermute | solution.py:418
  42.3 1.3 collective-permute-start.7
  43.6 0.0 collective-permute-done.right
  43.6 0.0 collective-permute-done.3.corner
  43.6 0.0 copy-done.6
  43.6 0.0 copy-done.7
  43.6 12.8 %shard_map.95 = (f32[8,2,256,256]{3,2,1,0:T(8,128)}, f32[8,256,256]{2,1,0:T(8,128)}) custom-call(s32[17]{0:T(128)} %pad_add_fusion.meta, f32[4,256,512]{2,1,0:T(8,128)} %own.5, f32[2,256,256]{2,1,0:T(8,128)} %collective-permute-done.right, f32[2,256,256]{2,1,0:T(8,128)} %copy-done.6, f32[2,256,256]{2,1,0:T(8,128)} %copy-done.7, ...), custom_call_target="tpu_custom_call" | custom-call | flops 6442450944 | bytes 12582912 | tf_op jit(solution)/shard_map/pallas_call | solution.py:383
  56.4 0.0 collective-permute-done.6.down1
  56.5 0.0 copy-start.8
  56.5 0.0 collective-permute-done.4.right
  56.5 0.0 collective-permute-done.7.corner
  56.5 0.0 copy-start.9
  56.5 0.8 copy-done.8
  57.3 0.2 copy-done.9
  57.5 13.4 %shard_map.96 = (f32[2,256,512]{2,1,0:T(8,128)}, f32[2,256,256]{2,1,0:T(8,128)}, f32[2,256,256]{2,1,0:T(8,128)}, f32[2,256,256]{2,1,0:T(8,128)}, f32[2,256,256]{2,1,0:T(8,128)}, /*index=5*/f32[8,2,256,256]{3,2,1,0:T(8,128)}) custom-call(s32[17]{0:T(128)} %pad_add_fusion.meta, f32[4,256,512]{2,1,0:T(8,128)} %own.5, ...), custom_call_target="tpu_custom_call" | custom-call | flops 6442450944 | bytes 12582912 | tf_op jit(solution)/shard_map/pallas_call | solution.py:394
  70.8 14.2 %shard_map.97 = (f32[2,256,512]{2,1,0:T(8,128)}, f32[2,256,256]{2,1,0:T(8,128)}, f32[2,256,256]{2,1,0:T(8,128)}, f32[2,256,256]{2,1,0:T(8,128)}, f32[2,256,256]{2,1,0:T(8,128)}, /*index=5*/f32[2,256,256]{2,1,0:T(8,128)}) custom-call(s32[17]{0:T(128)} %pad_add_fusion.meta, f32[4,256,512]{2,1,0:T(8,128)} %own.5, f32[2,256,256]{2,1,0:T(8,128)} %collective-permute-done.right, ...), custom_call_target="tpu_custom_call" | custom-call | flops 6442450944 | bytes 12582912 | tf_op jit(solution)/shard_map/pallas_call | solution.py:405
  85.1 0.0 copy-start.3
  85.1 1.5 collective-permute-start.9
  86.6 3.9 %collective-permute-start.13 = (f32[2,256,256]{2,1,0:T(8,128)}, f32[2,256,256]{2,1,0:T(8,128)}, u32[]{:S(2)}, u32[]{:S(2)}) collective-permute-start(f32[2,256,256]{2,1,0:T(8,128)} %get-tuple-element.27), channel_id=1, source_target_pairs={{0,1},{1,2},{2,3},{3,4},{4,5},{5,6},{6,7},{8,9},{9,10},{10,11},{11... | collective-permute-start | bytes 1572872 | tf_op jit(solution)/shard_map/ppermute | solution.py:418
  90.5 2.0 %reshape.15 = f32[128,4,256]{2,1,0:T(4,128)} reshape(f32[2,256,256]{2,1,0:T(8,128)} %get-tuple-element.29) | data formatting | bytes 1048576 | tf_op jit(solution)/shard_map/reshape | solution.py:440
  92.5 32.1 %all-to-all-start = ((f32[128,4,256]{2,1,0:T(4,128)}), f32[128,4,256]{2,1,0:T(4,128)S(1)}, u32[]{:S(2)}, u32[]{:S(2)}) async-start(f32[128,4,256]{2,1,0:T(4,128)} %reshape.15), calls=%async_computation | async-start | bytes 1048576 | tf_op jit(solution)/shard_map/all_to_all | solution.py:441
  124.6 2.1 %collective-permute-start.8 = (f32[2,256,256]{2,1,0:T(8,128)}, f32[2,256,256]{2,1,0:T(8,128)S(1)}, u32[]{:S(2)}, u32[]{:S(2)}) collective-permute-start(f32[2,256,256]{2,1,0:T(8,128)} %get-tuple-element.20), channel_id=1, source_target_pairs={{0,1},{1,2},{2,3},{3,4},{4,5},{5,6},{6,7},{8,9},{9,10},{10,11},{11... | collective-permute-start | bytes 1572872 | tf_op jit(solution)/shard_map/ppermute | solution.py:418
  126.7 3.5 %collective-permute-start.12 = (f32[2,256,256]{2,1,0:T(8,128)}, f32[2,256,256]{2,1,0:T(8,128)S(1)}, u32[]{:S(2)}, u32[]{:S(2)}) collective-permute-start(f32[2,256,256]{2,1,0:T(8,128)} %get-tuple-element.25), channel_id=1, source_target_pairs={{0,1},{1,2},{2,3},{3,4},{4,5},{5,6},{6,7},{8,9},{9,10},{10,11},{11... | collective-permute-start | bytes 1572872 | tf_op jit(solution)/shard_map/ppermute | solution.py:418
  130.2 0.0 collective-permute-done.9
  130.2 0.8 copy-done.4
  131.0 0.0 copy-done.3
  131.0 1.1 add.18
  132.2 3.4 %collective-permute-start.10 = (f32[2,256,256]{2,1,0:T(8,128)S(1)}, f32[2,256,256]{2,1,0:T(8,128)}, u32[]{:S(2)}, u32[]{:S(2)}) collective-permute-start(f32[2,256,256]{2,1,0:T(8,128)S(1)} %add.18), channel_id=1, source_target_pairs={{0,8},{8,16},{16,24},{24,32},{32,40},{40,48},{48,56},{56,64},{64,7... | collective-permute-start | bytes 1572872 | tf_op jit(solution)/shard_map/ppermute | solution.py:418
  135.6 0.0 collective-permute-done.13
  135.6 1.9 add.21
  137.5 3.4 %collective-permute-start.14 = (f32[2,256,256]{2,1,0:T(8,128)}, f32[2,256,256]{2,1,0:T(8,128)}, u32[]{:S(2)}, u32[]{:S(2)}) collective-permute-start(f32[2,256,256]{2,1,0:T(8,128)} %add.21), channel_id=1, source_target_pairs={{0,8},{8,16},{16,24},{24,32},{32,40},{40,48},{48,56},{56,64},{64,7... | collective-permute-start | bytes 1572872 | tf_op jit(solution)/shard_map/ppermute | solution.py:418
  141.0 3.1 %collective-permute-start.11 = (f32[2,256,256]{2,1,0:T(8,128)}, f32[2,256,256]{2,1,0:T(8,128)}, u32[]{:S(2)}, u32[]{:S(2)}) collective-permute-start(f32[2,256,256]{2,1,0:T(8,128)} %get-tuple-element.23), channel_id=1, source_target_pairs={{0,8},{8,16},{16,24},{24,32},{32,40},{40,48},{48,56},{56,64},{64,7... | collective-permute-start | bytes 1572872 | tf_op jit(solution)/shard_map/ppermute | solution.py:418
  144.1 0.0 all-to-all-done
  144.1 0.1 reduce_sum.9
  144.3 0.9 broadcast_in_dim.2
  145.2 9.1 %all-to-all-start.1 = ((f32[128,4,256]{2,1,0:T(4,128)}), f32[128,4,256]{2,1,0:T(4,128)S(1)}, u32[]{:S(2)}, u32[]{:S(2)}) async-start(f32[128,4,256]{2,1,0:T(4,128)} %broadcast_in_dim.2), calls=%async_computation.1 | async-start | bytes 1048576 | tf_op jit(solution)/shard_map/all_to_all | solution.py:443
  154.2 0.0 collective-permute-done.8
  154.2 0.0 copy-start.1
  154.3 3.5 %collective-permute-start.15 = (f32[2,256,256]{2,1,0:T(8,128)}, f32[2,256,256]{2,1,0:T(8,128)}, u32[]{:S(2)}, u32[]{:S(2)}) collective-permute-start(f32[2,256,256]{2,1,0:T(8,128)} %get-tuple-element.28), channel_id=1, source_target_pairs={{0,8},{8,16},{16,24},{24,32},{32,40},{40,48},{48,56},{56,64},{64,7... | collective-permute-start | bytes 1572872 | tf_op jit(solution)/shard_map/ppermute | solution.py:418
  157.8 27.4 %all-to-all-done.1 = f32[128,4,256]{2,1,0:T(4,128)S(1)} async-done(((f32[128,4,256]{2,1,0:T(4,128)}), f32[128,4,256]{2,1,0:T(4,128)S(1)}, u32[]{:S(2)}, u32[]{:S(2)}) %all-to-all-start.1) | async-done | bytes 524320 | tf_op jit(solution)/shard_map/all_to_all | solution.py:443
  185.2 1.0 reshape.16
  186.2 0.0 collective-permute-done.10
  186.2 1.1 add.19
  187.3 0.0 collective-permute-done.12
  187.3 0.0 collective-permute-done.14
  187.3 1.2 add.22
  188.5 0.0 collective-permute-done.11
  188.5 1.2 maximum_add_fusion
  189.8 3.3 %collective-permute-done.15 = f32[2,256,256]{2,1,0:T(8,128)} collective-permute-done((f32[2,256,256]{2,1,0:T(8,128)}, f32[2,256,256]{2,1,0:T(8,128)}, u32[]{:S(2)}, u32[]{:S(2)}) %collective-permute-start.15) | collective-permute-done | bytes 524320 | tf_op jit(solution)/shard_map/ppermute | solution.py:418
  193.1 1.2 maximum_add_fusion.1
  194.3 1.5 pad_maximum_fusion
  (9 shorter events, 0.0 us)
Async XLA Ops:
  0.6 22.4 %copy-start.5 = (s32[8,2]{0,1:T(2,128)S(1)}, s32[8,2]{0,1:T(2,128)}, u32[]{:S(2)}) copy-start(s32[8,2]{0,1:T(2,128)} %param.10) | copy-start | bytes 196
  2.3 17.5 %collective-permute-start.1 = (f32[2,256,256]{2,1,0:T(8,128)S(1)}, f32[2,256,256]{2,1,0:T(8,128)S(1)}, u32[]{:S(2)}, u32[]{:S(2)}) collective-permute-start(f32[2,256,256]{2,1,0:T(8,128)S(1)} %get-tuple-element.33), channel_id=1, source_target_pairs={{8,0},{16,8},{24,16},{32,24},{40,32},{48,40},{56,48},{64,56},{72,6... | collective-permute-start | bytes 1572872 | tf_op jit(solution)/shard_map/ppermute | solution.py:418
  7.5 23.5 %collective-permute-start.2 = (f32[2,256,256]{2,1,0:T(8,128)S(1)}, f32[2,256,256]{2,1,0:T(8,128)S(1)}, u32[]{:S(2)}, u32[]{:S(2)}) collective-permute-start(f32[2,256,256]{2,1,0:T(8,128)S(1)} %get-tuple-element.30), channel_id=1, source_target_pairs={{8,0},{16,8},{24,16},{32,24},{40,32},{48,40},{56,48},{64,56},{72,6... | collective-permute-start | bytes 1572872 | tf_op jit(solution)/shard_map/ppermute | solution.py:418
  10.2 32.1 %collective-permute-start.5 = (f32[2,256,256]{2,1,0:T(8,128)S(1)}, f32[2,256,256]{2,1,0:T(8,128)}, u32[]{:S(2)}, u32[]{:S(2)}) collective-permute-start(f32[2,256,256]{2,1,0:T(8,128)S(1)} %get-tuple-element.32), channel_id=1, source_target_pairs={{8,0},{16,8},{24,16},{32,24},{40,32},{48,40},{56,48},{64,56},{72,6... | collective-permute-start | bytes 1572872 | tf_op jit(solution)/shard_map/ppermute | solution.py:418
  12.5 31.0 %collective-permute-start = (f32[2,256,256]{2,1,0:T(8,128)S(1)}, f32[2,256,256]{2,1,0:T(8,128)}, u32[]{:S(2)}, u32[]{:S(2)}) collective-permute-start(f32[2,256,256]{2,1,0:T(8,128)S(1)} %get-tuple-element.33), channel_id=1, source_target_pairs={{1,0},{2,1},{3,2},{4,3},{5,4},{6,5},{7,6},{9,8},{10,9},{11,10},{12... | collective-permute-start | bytes 1572872 | tf_op jit(solution)/shard_map/ppermute | solution.py:418
  19.8 23.8 %copy-start.6 = (f32[2,256,256]{2,1,0:T(8,128)}, f32[2,256,256]{2,1,0:T(8,128)S(1)}, u32[]{:S(2)}) copy-start(f32[2,256,256]{2,1,0:T(8,128)S(1)} %collective-permute-done.1.down0) | copy-start | bytes 1572868
  19.8 23.8 %collective-permute-start.3 = (f32[2,256,256]{2,1,0:T(8,128)S(1)}, f32[2,256,256]{2,1,0:T(8,128)}, u32[]{:S(2)}, u32[]{:S(2)}) collective-permute-start(f32[2,256,256]{2,1,0:T(8,128)S(1)} %collective-permute-done.1.down0), channel_id=1, source_target_pairs={{1,0},{2,1},{3,2},{4,3},{5,4},{6,5},{7,6},{9,8},{10,9},{11,10},{12... | collective-permute-start | bytes 1572872 | tf_op jit(solution)/shard_map/ppermute | solution.py:418
  21.1 35.4 %collective-permute-start.4 = (f32[2,256,256]{2,1,0:T(8,128)S(1)}, f32[2,256,256]{2,1,0:T(8,128)}, u32[]{:S(2)}, u32[]{:S(2)}) collective-permute-start(f32[2,256,256]{2,1,0:T(8,128)S(1)} %get-tuple-element.32), channel_id=1, source_target_pairs={{1,0},{2,1},{3,2},{4,3},{5,4},{6,5},{7,6},{9,8},{10,9},{11,10},{12... | collective-permute-start | bytes 1572872 | tf_op jit(solution)/shard_map/ppermute | solution.py:418
  31.0 12.6 %copy-start.7 = (f32[2,256,256]{2,1,0:T(8,128)}, f32[2,256,256]{2,1,0:T(8,128)S(1)}, u32[]{:S(2)}) copy-start(f32[2,256,256]{2,1,0:T(8,128)S(1)} %collective-permute-done.2.down1) | copy-start | bytes 1572868
  31.0 25.4 %collective-permute-start.6 = (f32[2,256,256]{2,1,0:T(8,128)S(1)}, f32[2,256,256]{2,1,0:T(8,128)S(1)}, u32[]{:S(2)}, u32[]{:S(2)}) collective-permute-start(f32[2,256,256]{2,1,0:T(8,128)S(1)} %get-tuple-element.31), channel_id=1, source_target_pairs={{8,0},{16,8},{24,16},{32,24},{40,32},{48,40},{56,48},{64,56},{72,6... | collective-permute-start | bytes 1572872 | tf_op jit(solution)/shard_map/ppermute | solution.py:418
  42.3 14.2 %collective-permute-start.7 = (f32[2,256,256]{2,1,0:T(8,128)}, f32[2,256,256]{2,1,0:T(8,128)S(1)}, u32[]{:S(2)}, u32[]{:S(2)}) collective-permute-start(f32[2,256,256]{2,1,0:T(8,128)} %collective-permute-done.5.down0), channel_id=1, source_target_pairs={{1,0},{2,1},{3,2},{4,3},{5,4},{6,5},{7,6},{9,8},{10,9},{11,10},{12... | collective-permute-start | bytes 1572872 | tf_op jit(solution)/shard_map/ppermute | solution.py:418
  56.5 0.8 copy-start.8
  56.5 1.0 copy-start.9
  85.1 46.0 %copy-start.3 = (f32[2,256,256]{2,1,0:T(8,128)S(1)}, f32[2,256,256]{2,1,0:T(8,128)}, u32[]{:S(2)}) copy-start(f32[2,256,256]{2,1,0:T(8,128)} %get-tuple-element.21) | copy-start | bytes 1572868
  85.1 50.5 %copy-start.2 = (f32[2,256,256]{2,1,0:T(8,128)S(1)}, f32[2,256,256]{2,1,0:T(8,128)}, u32[]{:S(2)}) copy-start(f32[2,256,256]{2,1,0:T(8,128)} %get-tuple-element.26) | copy-start | bytes 1572868
  85.1 45.1 %collective-permute-start.9 = (f32[2,256,256]{2,1,0:T(8,128)}, f32[2,256,256]{2,1,0:T(8,128)S(1)}, u32[]{:S(2)}, u32[]{:S(2)}) collective-permute-start(f32[2,256,256]{2,1,0:T(8,128)} %get-tuple-element.22), channel_id=1, source_target_pairs={{0,1},{1,2},{2,3},{3,4},{4,5},{5,6},{6,7},{8,9},{9,10},{10,11},{11... | collective-permute-start | bytes 1572872 | tf_op jit(solution)/shard_map/ppermute | solution.py:418
  86.6 49.0 %collective-permute-start.13 = (f32[2,256,256]{2,1,0:T(8,128)}, f32[2,256,256]{2,1,0:T(8,128)}, u32[]{:S(2)}, u32[]{:S(2)}) collective-permute-start(f32[2,256,256]{2,1,0:T(8,128)} %get-tuple-element.27), channel_id=1, source_target_pairs={{0,1},{1,2},{2,3},{3,4},{4,5},{5,6},{6,7},{8,9},{9,10},{10,11},{11... | collective-permute-start | bytes 1572872 | tf_op jit(solution)/shard_map/ppermute | solution.py:418
  92.5 51.6 %all-to-all-start = ((f32[128,4,256]{2,1,0:T(4,128)}), f32[128,4,256]{2,1,0:T(4,128)S(1)}, u32[]{:S(2)}, u32[]{:S(2)}) async-start(f32[128,4,256]{2,1,0:T(4,128)} %reshape.15), calls=%async_computation | async-start | bytes 1048576 | tf_op jit(solution)/shard_map/all_to_all | solution.py:441
  124.6 29.6 %collective-permute-start.8 = (f32[2,256,256]{2,1,0:T(8,128)}, f32[2,256,256]{2,1,0:T(8,128)S(1)}, u32[]{:S(2)}, u32[]{:S(2)}) collective-permute-start(f32[2,256,256]{2,1,0:T(8,128)} %get-tuple-element.20), channel_id=1, source_target_pairs={{0,1},{1,2},{2,3},{3,4},{4,5},{5,6},{6,7},{8,9},{9,10},{10,11},{11... | collective-permute-start | bytes 1572872 | tf_op jit(solution)/shard_map/ppermute | solution.py:418
  126.7 60.6 %collective-permute-start.12 = (f32[2,256,256]{2,1,0:T(8,128)}, f32[2,256,256]{2,1,0:T(8,128)S(1)}, u32[]{:S(2)}, u32[]{:S(2)}) collective-permute-start(f32[2,256,256]{2,1,0:T(8,128)} %get-tuple-element.25), channel_id=1, source_target_pairs={{0,1},{1,2},{2,3},{3,4},{4,5},{5,6},{6,7},{8,9},{9,10},{10,11},{11... | collective-permute-start | bytes 1572872 | tf_op jit(solution)/shard_map/ppermute | solution.py:418
  130.2 0.8 copy-start.4
  132.2 54.0 %collective-permute-start.10 = (f32[2,256,256]{2,1,0:T(8,128)S(1)}, f32[2,256,256]{2,1,0:T(8,128)}, u32[]{:S(2)}, u32[]{:S(2)}) collective-permute-start(f32[2,256,256]{2,1,0:T(8,128)S(1)} %add.18), channel_id=1, source_target_pairs={{0,8},{8,16},{16,24},{24,32},{32,40},{40,48},{48,56},{56,64},{64,7... | collective-permute-start | bytes 1572872 | tf_op jit(solution)/shard_map/ppermute | solution.py:418
  137.5 49.8 %collective-permute-start.14 = (f32[2,256,256]{2,1,0:T(8,128)}, f32[2,256,256]{2,1,0:T(8,128)}, u32[]{:S(2)}, u32[]{:S(2)}) collective-permute-start(f32[2,256,256]{2,1,0:T(8,128)} %add.21), channel_id=1, source_target_pairs={{0,8},{8,16},{16,24},{24,32},{32,40},{40,48},{48,56},{56,64},{64,7... | collective-permute-start | bytes 1572872 | tf_op jit(solution)/shard_map/ppermute | solution.py:418
  141.0 47.5 %collective-permute-start.11 = (f32[2,256,256]{2,1,0:T(8,128)}, f32[2,256,256]{2,1,0:T(8,128)}, u32[]{:S(2)}, u32[]{:S(2)}) collective-permute-start(f32[2,256,256]{2,1,0:T(8,128)} %get-tuple-element.23), channel_id=1, source_target_pairs={{0,8},{8,16},{16,24},{24,32},{32,40},{40,48},{48,56},{56,64},{64,7... | collective-permute-start | bytes 1572872 | tf_op jit(solution)/shard_map/ppermute | solution.py:418
  145.2 40.0 %all-to-all-start.1 = ((f32[128,4,256]{2,1,0:T(4,128)}), f32[128,4,256]{2,1,0:T(4,128)S(1)}, u32[]{:S(2)}, u32[]{:S(2)}) async-start(f32[128,4,256]{2,1,0:T(4,128)} %broadcast_in_dim.2), calls=%async_computation.1 | async-start | bytes 1048576 | tf_op jit(solution)/shard_map/all_to_all | solution.py:443
  154.2 34.3 %copy-start.1 = (f32[2,256,512]{2,1,0:T(8,128)S(1)}, f32[2,256,512]{2,1,0:T(8,128)}, u32[]{:S(2)}) copy-start(f32[2,256,512]{2,1,0:T(8,128)} %get-tuple-element.19) | copy-start | bytes 3145732
  154.3 38.8 %collective-permute-start.15 = (f32[2,256,256]{2,1,0:T(8,128)}, f32[2,256,256]{2,1,0:T(8,128)}, u32[]{:S(2)}, u32[]{:S(2)}) collective-permute-start(f32[2,256,256]{2,1,0:T(8,128)} %get-tuple-element.28), channel_id=1, source_target_pairs={{0,8},{8,16},{16,24},{24,32},{32,40},{40,48},{48,56},{56,64},{64,7... | collective-permute-start | bytes 1572872 | tf_op jit(solution)/shard_map/ppermute | solution.py:418
  187.3 5.8 %copy-start = (f32[2,256,512]{2,1,0:T(8,128)S(1)}, f32[2,256,512]{2,1,0:T(8,128)}, u32[]{:S(2)}) copy-start(f32[2,256,512]{2,1,0:T(8,128)} %get-tuple-element.24) | copy-start | bytes 3145732
